TPU v7x, 32 devices: a whole 2x2x4 slice. The times are simulated.
32 devices in a mesh: pair: 16 (over z, y, x), aux: 2 (over core).
Axes of the slice: x: 2, y: 2, z: 4, core: 2. Of those that a mesh axis runs over, the one named last changes fastest.
Arguments:
- amplitudes: bfloat16 [2048, 128, 128], P('pair', 'aux'), may hold values from -6 to 6
- k_term: bfloat16 [2048, 128, 128], P('pair', 'aux'), may hold values from -6 to 6
- margin_table: bfloat16 [128, 128, 128], P('pair'), may hold values from -0.5 to 0.5
- margin_index: int32 [2048], P('pair'), may hold values from 0 to 7
- factors: bfloat16 [16, 512, 128], P('pair', 'aux'), may hold values from -6 to 6
- vir_energy: float32 [2048, 128], P('pair'), may hold values from 0.5 to 3
- occ_energy: float32 [16], replicated, may hold values from -2 to -0.3
- pair_owner: int32 [2048, 1], P('pair'), may hold values from 0 to 15; in each aligned block of 128 rows (0 to 127, 128 to 255, ...) at most 16 rows name the same one
Outputs:
- updated: bfloat16 [2048, 128, 128], P('pair', 'aux')
Inputs may be any that keep to these rules, and one draw needn't show every extreme that they name: `pair_owner`: no more than 16 of the 128 pairs of one aligned block name the same owner. `margin_index`: an index into the 8 margin blocks that belong to the pair's aligned block of 128 pairs.
All inputs are finite; a program needn't handle non-finite values.
Results may differ from a plain program's by a relative error of at most 0.0055.
Values may be sent and summed in bfloat16 or wider, within the bound.
A program may use at most 128 MiB of HBM per device.

v0:
```python
import jax
import jax.numpy as jnp
from jax import lax
from jax.sharding import PartitionSpec as P


def local(
    amplitudes, k_term, margin_table, margin_index, factors, vir_energy, occ_energy, pair_owner
):
    axis_pairs = lax.axis_size("pair")
    aux_count = lax.axis_size("aux")
    own_index = lax.axis_index("pair")
    aux_index = lax.axis_index("aux")
    pair_count = amplitudes.shape[0]
    row_count = amplitudes.shape[1]
    vir_width = amplitudes.shape[2]
    aux_rows = factors.shape[1]
    ovl_count = margin_table.shape[0]
    capacity = max(2, (2 * pair_count + axis_pairs - 1) // axis_pairs)
    cycle_scale = float(vir_width * aux_rows * aux_count * pair_count) ** (-0.5)
    own_factors = factors[0]
    full_amp = lax.all_gather(amplitudes, "aux", axis=1, tiled=True)
    block_pick = (margin_index[:, None] == jnp.arange(ovl_count, dtype=jnp.int32)[None, :]).astype(
        jnp.bfloat16
    )
    margin = jnp.einsum(
        "po,oab->pab", block_pick, margin_table, preferred_element_type=jnp.float32
    ).astype(jnp.bfloat16)
    halfway = jnp.einsum(
        "pca,pab->pcb", full_amp, margin, preferred_element_type=jnp.float32
    ).astype(jnp.bfloat16)
    rotated = jnp.einsum(
        "pac,pab->pcb", margin, halfway, preferred_element_type=jnp.float32
    ).astype(jnp.bfloat16)
    partial_value = jnp.einsum(
        "pca,qa->pcq", rotated, own_factors, preferred_element_type=jnp.float32
    ).astype(jnp.bfloat16)
    pair_dest = pair_owner[:, 0]
    owner_hits = (pair_dest[:, None] == jnp.arange(axis_pairs, dtype=jnp.int32)[None, :]).astype(
        jnp.int32
    )
    slot_rank = jnp.sum(jnp.cumsum(owner_hits, axis=0) * owner_hits, axis=1) - 1
    slot_index = pair_dest * capacity + slot_rank
    outgoing = (
        jnp.zeros((axis_pairs * capacity, vir_width, aux_rows), jnp.bfloat16)
        .at[slot_index]
        .set(partial_value)
    )
    outgoing = outgoing.reshape(axis_pairs, capacity, vir_width, aux_rows)
    incoming = lax.all_to_all(outgoing, "pair", split_axis=0, concat_axis=0, tiled=True)
    slot_ones = jnp.ones((axis_pairs, capacity), jnp.bfloat16)
    summed = jnp.einsum(
        "sk,skcq->cq", slot_ones, incoming, preferred_element_type=jnp.float32
    ).astype(jnp.bfloat16)
    local_cycle = jnp.dot(summed, own_factors, preferred_element_type=jnp.float32)
    cycle_sum = lax.psum(local_cycle, "aux")
    cycle_vals = (cycle_scale * cycle_sum).astype(jnp.bfloat16)
    cycle_rows = cycle_vals.shape[0]
    slot_back = jnp.broadcast_to(
        cycle_vals[None, None], (axis_pairs, capacity, cycle_rows, vir_width)
    )
    returned = lax.all_to_all(slot_back, "pair", split_axis=0, concat_axis=0, tiled=True)
    own_cycle = returned.reshape(axis_pairs * capacity, cycle_rows, vir_width)[slot_index]
    own_cycle = lax.dynamic_slice_in_dim(own_cycle, aux_index * row_count, row_count, 1)
    cycle_term = jnp.einsum("pca,pba->pcb", own_cycle, margin, preferred_element_type=jnp.float32)
    occ_total = occ_energy.shape[0]
    occ_first = jnp.zeros((pair_count,), jnp.int32) + own_index
    both_ids = jnp.concatenate([occ_first, pair_dest])
    occ_select = (both_ids[:, None] == jnp.arange(occ_total, dtype=jnp.int32)[None, :]).astype(
        jnp.float32
    )
    occ_values = jnp.sum(occ_select * occ_energy[None, :], axis=1)
    occ_sum = occ_values[:pair_count] + occ_values[pair_count:]
    energy_rows = lax.dynamic_slice_in_dim(vir_energy, aux_index * row_count, row_count, 1)
    denominator = energy_rows[:, :, None] + vir_energy[:, None, :] - occ_sum[:, None, None]
    updated = (
        amplitudes.astype(jnp.float32) - (cycle_term + k_term.astype(jnp.float32)) / denominator
    )
    return updated.astype(jnp.bfloat16)


def solution(mesh):
    placed = (
        P("pair", "aux", None),
        P("pair", "aux", None),
        P("pair", None, None),
        P("pair"),
        P("pair", "aux", None),
        P("pair", None),
        P(),
        P("pair", None),
    )
    return jax.shard_map(
        local, mesh=mesh, in_specs=placed, out_specs=P("pair", "aux", None), check_vma=False
    )
```

profile of v0, /device:TPU:28, one launch (start us, length us, event | category | flops | bytes accessed | tf_op | source)
XLA Modules:
  0.0 697.3 jit_solution(17998518379526050553)
XLA Ops:
  6.5 0.0 copy-start
  6.5 0.0 all-gather.2.cloned.1.call-start
  6.5 0.7 all-gather.2.cloned.1.call-update
  7.3 0.0 all-reduce.3.cloned.1.call-start
  7.3 0.7 fusion.24
  8.1 0.2 reduce_window_sum.11
  8.2 0.8 select_reduce_fusion
  9.1 0.7 fusion.29
  9.7 0.0 copy-done
  9.7 3.9 convolution_convert_fusion.1
  13.6 0.0 copy-start.3
  13.6 10.2 %all-gather.2.cloned.1.call-done = bf16[128,128,128]{2,1,0:T(8,128)(2,1)} async-done(((bf16[128,64,128]{2,1,0:T(8,128)(2,1)}), bf16[128,128,128]{2,1,0:T(8,128)(2,1)}) %all-gather.2.cloned.1.call-update) | async-done | bytes 4194320 | tf_op jit(solution)/shard_map/all_gather | solution.py:22
  23.8 9.4 %fusion.11 = bf16[128,128,128]{2,1,0:T(8,128)(2,1)} fusion(bf16[128,128,128]{2,1,0:T(8,128)(2,1)} %all-gather.2.cloned.1.call-done, bf16[128,128,128]{2,0,1:T(8,128)(2,1)} %convolution_convert_fusion.1), kind=kOutput, calls=%fused_computation.10 | convolution fusion | flops 536870912 | bytes 12582912 | tf_op jit(solution)/shard_map/pca,pab->pcb/dot_general | solution.py:29
  33.2 0.0 copy-done.3
  33.2 11.1 %convolution_convert_fusion = bf16[128,128,256]{2,1,0:T(8,128)(2,1)} fusion(bf16[128,128,128]{2,1,0:T(8,128)(2,1)} %fusion.11, bf16[128,128,128]{2,0,1:T(8,128)(2,1)} %convolution_convert_fusion.1, bf16[1,256,128]{2,1,0:T(8,128)(2,1)S(1)} %copy-done.3), kind=kOutput, calls=%fused_computation.4 | convolution fusion | flops 1616904192 | bytes 16842752 | tf_op jit(solution)/shard_map/pca,qa->pcq/dot_general | solution.py:35
  44.2 6.0 broadcast_in_dim.7
  50.2 23.5 %scatter_fusion = bf16[256,128,256]{2,1,0:T(8,128)(2,1)} fusion(bf16[256,128,256]{2,1,0:T(8,128)(2,1)} %broadcast_in_dim.7, s32[128]{0:T(128)S(1)} %fusion.29, bf16[128,128,256]{2,1,0:T(8,128)(2,1)} %convolution_convert_fusion), kind=kCustom, calls=%fused_computation.1 | custom fusion | bytes 25166336 | tf_op jit(solution)/shard_map/scatter | solution.py:47
  73.7 368.6 %all_to_all.10 = bf16[16,16,128,256]{3,2,1,0:T(8,128)(2,1)S(1)} all-to-all(bf16[16,16,128,256]{3,2,1,0:T(8,128)(2,1)} %bitcast.23), channel_id=1, replica_groups=mesh['pair'=16,'aux'=2] {'pair'}, dimensions={0} | all-to-all | bytes 33554432 | tf_op jit(solution)/shard_map/all_to_all | solution.py:50
  442.3 9.7 %fusion = bf16[1,128,256,1]{2,0,3,1:T(2,128)(2,1)S(1)} fusion(bf16[16,16,128,256]{3,2,1,0:T(8,128)(2,1)S(1)} %all_to_all.10), kind=kOutput, calls=%fused_computation.2 | convolution fusion | flops 16777216 | bytes 16842752 | tf_op jit(solution)/shard_map/sk,skcq->cq/dot_general | solution.py:52
  452.0 0.8 fusion.21
  452.8 0.0 all-reduce.3.cloned.1.call-update
  452.8 18.1 %all-reduce.3.cloned.1.call-done = f32[128,128]{1,0:T(8,128)} async-done(((f32[128,128]{1,0:T(8,128)}), f32[128,128]{1,0:T(8,128)}) %all-reduce.3.cloned.1.call-update) | async-done | bytes 65552 | tf_op jit(solution)/shard_map/psum | solution.py:56
  471.0 0.8 multiply_convert_fusion
  471.8 5.3 broadcast_in_dim.8
  477.2 0.0 copy-start.5
  477.2 0.0 copy-start.6
  477.2 0.0 copy-start.4
  477.2 7.1 %all-to-all-start.1 = ((bf16[16,16,128,128]{3,2,1,0:T(8,128)(2,1)}), bf16[16,16,128,128]{3,2,1,0:T(8,128)(2,1)}, u32[]{:S(2)}, u32[]{:S(2)}) async-start(bf16[16,16,128,128]{3,2,1,0:T(8,128)(2,1)} %broadcast_in_dim.8), calls=%async_computation.1 | async-start | bytes 16777216 | tf_op jit(solution)/shard_map/all_to_all | solution.py:62
  484.2 0.0 copy-done.5
  484.3 0.0 copy-done.6
  484.3 0.1 select_reduce_fusion.1
  484.4 0.0 copy-done.4
  484.4 0.1 constant_dynamic-slice_fusion
  484.4 190.8 %all-to-all-done.1 = bf16[16,16,128,128]{3,2,1,0:T(8,128)(2,1)} async-done(((bf16[16,16,128,128]{3,2,1,0:T(8,128)(2,1)}), bf16[16,16,128,128]{3,2,1,0:T(8,128)(2,1)}, u32[]{:S(2)}, u32[]{:S(2)}) %all-to-all-start.1) | async-done | bytes 8388640 | tf_op jit(solution)/shard_map/all_to_all | solution.py:62
  675.3 0.0 copy-start.2
  675.3 6.6 gather_fusion
  681.8 0.0 copy-done.2
  681.8 0.0 copy-start.1
  681.8 8.6 %subtract_convert_fusion = bf16[128,64,128]{2,1,0:T(8,128)(2,1)} fusion(bf16[128,64,128]{2,1,0:T(8,128)(2,1)} %param.9, bf16[128,64,128]{2,1,0:T(8,128)(2,1)S(1)} %copy-done.2, f32[128]{0:T(128)S(1)} %slice_add_fusion, f32[128,128]{1,0:T(8,128)S(1)} %copy-done.4, f32[128,64]{1,0:T(8,128)S(1)} %constant_dynamic-slice_fusion, ...), kind=kOutput, calls=%fused_computation.5 | convolution fusion | flops 276824064 | bytes 12681732 | tf_op jit(solution)/shard_map/pca,pba->pcb/dot_general | solution.py:65
  690.5 0.0 copy-done.1
  (3 shorter events, 0.0 us)
Async XLA Ops:
  6.5 3.2 copy-start
  6.5 17.3 %all-gather.2.cloned.1.call-start = ((), (), s32[]{:S(2)}) async-start(), calls=%async_computation.2 | async-start | bytes 6291456 | tf_op jit(solution)/shard_map/all_gather | solution.py:22
  7.3 463.7 %all-reduce.3.cloned.1.call-start = ((), (), s32[]{:S(2)}) async-start(), calls=%async_computation.3 | async-start | bytes 131072 | tf_op jit(solution)/shard_map/psum | solution.py:56
  13.6 19.6 %copy-start.3 = (bf16[1,256,128]{2,1,0:T(8,128)(2,1)S(1)}, bf16[1,256,128]{2,1,0:T(8,128)(2,1)}, u32[]{:S(2)}) copy-start(bf16[1,256,128]{2,1,0:T(8,128)(2,1)} %param.12) | copy-start | bytes 196612
  477.2 7.1 %copy-start.5 = (s32[128,1]{0,1:T(1,128)S(1)}, s32[128,1]{0,1:T(1,128)}, u32[]{:S(2)}) copy-start(s32[128,1]{0,1:T(1,128)} %param.15) | copy-start | bytes 1540
  477.2 7.1 %copy-start.6 = (f32[16]{0:T(128)S(1)}, f32[16]{0:T(128)}, u32[]{:S(2)}) copy-start(f32[16]{0:T(128)} %param.14) | copy-start | bytes 196
  477.2 7.2 %copy-start.4 = (f32[128,128]{1,0:T(8,128)S(1)}, f32[128,128]{1,0:T(8,128)}, u32[]{:S(2)}) copy-start(f32[128,128]{1,0:T(8,128)} %param.13) | copy-start | bytes 196612
  477.2 198.1 %all-to-all-start.1 = ((bf16[16,16,128,128]{3,2,1,0:T(8,128)(2,1)}), bf16[16,16,128,128]{3,2,1,0:T(8,128)(2,1)}, u32[]{:S(2)}, u32[]{:S(2)}) async-start(bf16[16,16,128,128]{3,2,1,0:T(8,128)(2,1)} %broadcast_in_dim.8), calls=%async_computation.1 | async-start | bytes 16777216 | tf_op jit(solution)/shard_map/all_to_all | solution.py:62
  675.3 6.6 copy-start.2
  681.8 8.6 %copy-start.1 = (bf16[8,128,128]{2,1,0:T(8,128)(2,1)S(1)}, bf16[8,128,128]{2,1,0:T(8,128)(2,1)}, u32[]{:S(2)}) copy-start(bf16[8,128,128]{2,1,0:T(8,128)(2,1)} %param.10) | copy-start | bytes 786436
Sparse Core Ops, SparseCore 0:
  8.9 14.8 all-gather.1
  453.0 17.9 all-reduce.2
where the time goes:
time: 698 us; the launch traced here: 697 us
  blocking collectives  369 us (53%)
  waiting for transfers between devices  220 us (32%)
  matrix products  43.5 us (6%)
  local copies, waits for them, and re-layouts  41.5 us (6%)
  between operations  13.5 us (2%)
  starting transfers between devices  7.09 us (1%)
    all_to_all x1, blocking collectives, local(): lax.all_to_all(outgoing, 'pair', split_axis=0, concat_axis=0, tiled=True)  369 us
    all_to_all x1, waiting for transfers between devices, local(): lax.all_to_all(slot_back, 'pair', split_axis=0, concat_axis=0, tiled=True)  191 us
    scatter x1, local copies, waits for them, and re-layouts, local(): outgoing = jnp.zeros((axis_pairs * capacity, vir_width, aux_rows), jnp.bf...  23.5 us
    psum x1, waiting for transfers between devices, local(): cycle_sum = lax.psum(local_cycle, 'aux')  18.1 us
  transfers between devices with their start and end apart: 3, of which 3 were waited for; matrix products, arithmetic and copies ran while one was open for 1% of the time, Pallas kernels for 0%

commit v1 on v0

v1 whole, which is shorter than its diff:
```python
import functools

import jax
import jax.numpy as jnp
from jax import lax
from jax.experimental import pallas as pl
from jax.experimental.pallas import tpu as pltpu
from jax.sharding import PartitionSpec as P

MESH = pl.DeviceIdType.MESH
VMEM_BYTES = 56 * 1024 * 1024
GROUP = 16
CHUNKS = 4


def dot(a, b):
    return jnp.dot(a, b, preferred_element_type=jnp.float32)


def cycle_kernel(
    sizes, scale,
    last_ref, amp_hbm, fac_hbm, table_ref, cyc_out,
    amp, prefix, stacked, half, margin_t, r_send, r_own, r_recv, r_sum, r_in,
    f_plane, f_col, g_own, g_send, g_recv, g_sum, c_own, c_send, c_recv, cyc,
    amp_sem, loc_sem, fp_s, fp_r, fz_s, fz_r, sib_s, sib_r, r_s, r_r, c_s, c_r, az_s, ap_s, ag_r,
):
    count, planes, cols, tables = sizes
    rows = amp.shape[1]
    pairs = amp.shape[0]
    me, h = lax.axis_index("pair"), lax.axis_index("aux")
    col, plane = lax.div(me, planes), lax.rem(me, planes)
    sibling = (me, 1 - h)
    plane_peers = [lax.rem(plane + d, planes) for d in range(1, planes)]
    col_peers = [lax.rem(col + d, cols) for d in range(1, cols)]

    def at_plane(t):
        return (col * planes + t, h)

    def at_col(z):
        return (z * planes + plane, h)

    def remote(src, dst, send, recv, device):
        return pltpu.make_async_remote_copy(
            src_ref=src, dst_ref=dst, send_sem=send, recv_sem=recv,
            device_id=device, device_id_type=MESH,
        )

    step = pairs // CHUNKS
    loads = []
    for k in range(CHUNKS):
        part = pl.ds(k * step, step)
        loads.append(pltpu.make_async_copy(amp_hbm.at[part], amp.at[part], amp_sem.at[k]))
        loads[-1].start()
    own_plane = pltpu.make_async_copy(fac_hbm.at[0], f_plane.at[plane], loc_sem.at[0])
    own_col = pltpu.make_async_copy(fac_hbm.at[0], f_col.at[col], loc_sem.at[1])
    own_plane.start()
    own_col.start()

    barrier = pltpu.get_barrier_semaphore()
    for device in [sibling] + [at_plane(t) for t in plane_peers] + [at_col(z) for z in col_peers]:
        pl.semaphore_signal(barrier, inc=1, device_id=device, device_id_type=MESH)
    pl.semaphore_wait(barrier, 1 + (planes - 1) + (cols - 1))

    sends = []
    for z in col_peers:
        sends.append(remote(fac_hbm.at[0], f_col.at[col], fz_s.at[z], fz_r.at[col], at_col(z)))
        sends[-1].start()
    for t in plane_peers:
        sends.append(remote(fac_hbm.at[0], f_plane.at[plane], fp_s.at[t], fp_r.at[plane], at_plane(t)))
        sends[-1].start()

    prefix[pairs] = jnp.zeros(prefix.shape[1:], jnp.float32)
    for m in range(tables):
        piece = table_ref[m, pl.ds(pl.multiple_of(h * rows, rows), rows), :]
        margin_t[:, m * rows : (m + 1) * rows] = piece.T

    for k in range(CHUNKS):
        loads[k].wait()

        def add_pair(p, carry):
            prefix[p] = amp[p].astype(jnp.float32) + prefix[last_ref[p]]
            return carry

        lax.fori_loop(k * step, (k + 1) * step, add_pair, 0, unroll=4)

    other = margin_t[pl.ds(pl.multiple_of((1 - h) * rows, rows), rows), :]
    mine = margin_t[pl.ds(pl.multiple_of(h * rows, rows), rows), :]

    def rotate(g, carry):
        base = g * GROUP
        for m in range(tables):
            for o in range(GROUP):
                found = last_ref[pairs + (base + o) * tables + m]
                stacked[m, o * rows : (o + 1) * rows, :] = prefix[found].astype(jnp.bfloat16)
        for m in range(tables):
            for o in range(0, GROUP, 4):
                value = dot(stacked[m, o * rows : (o + 4) * rows, :], table_ref[m]).astype(jnp.bfloat16)
                for u in range(4):
                    half[m * rows : (m + 1) * rows, (o + u) * 128 : (o + u + 1) * 128] = value[
                        u * rows : (u + 1) * rows
                    ]
        for o in range(0, GROUP, 2):
            value = dot(other, half[:, o * 128 : (o + 2) * 128])
            for u in range(2):
                r_send[base + o + u] = value[:, u * 128 : (u + 1) * 128].astype(jnp.bfloat16)
        for o in range(0, GROUP, 2):
            value = dot(mine, half[:, o * 128 : (o + 2) * 128])
            for u in range(2):
                r_own[base + o + u] = value[:, u * 128 : (u + 1) * 128]
        return carry

    lax.fori_loop(0, count // GROUP, rotate, 0)

    swap_r = remote(r_send, r_recv, sib_s.at[0], sib_r.at[0], sibling)
    swap_r.start()

    own_plane.wait()
    own_col.wait()
    for t in plane_peers:
        remote(fac_hbm.at[0], f_plane.at[t], fp_s.at[t], fp_r.at[t], at_plane(t)).wait_recv()
    for z in col_peers:
        remote(fac_hbm.at[0], f_col.at[z], fz_s.at[z], fz_r.at[z], at_col(z)).wait_recv()

    def metric(z, carry):
        for s in range(planes):
            value = dot(f_plane[s].T, f_col[z])
            g_own[z, s * 128 : (s + 1) * 128, :] = value
            g_send[z, s * 128 : (s + 1) * 128, :] = value.astype(jnp.bfloat16)
        return carry

    lax.fori_loop(0, cols, metric, 0)
    swap_g = remote(g_send, g_recv, sib_s.at[1], sib_r.at[1], sibling)
    swap_g.start()

    swap_r.wait()
    r_sum[...] = (r_own[...] + r_recv[...].astype(jnp.float32)).astype(jnp.bfloat16)
    for t in plane_peers:
        sends.append(
            remote(
                r_sum.at[pl.ds(t * cols, cols)], r_in.at[plane], r_s.at[t], r_r.at[plane], at_plane(t)
            )
        )
        sends[-1].start()
    r_in[plane] = r_sum[pl.ds(plane * cols, cols)]
    swap_g.wait()
    g_sum[...] = (g_own[...] + g_recv[...].astype(jnp.float32)).astype(jnp.bfloat16)
    for t in plane_peers:
        remote(
            r_sum.at[pl.ds(t * cols, cols)], r_in.at[t], r_s.at[t], r_r.at[t], at_plane(t)
        ).wait_recv()

    def contract(z, carry):
        left = jnp.concatenate([r_in[s, z] for s in range(planes)], axis=1)
        value = dot(left, g_sum[z])
        c_own[z] = value
        c_send[z] = value.astype(jnp.bfloat16)
        return carry

    lax.fori_loop(0, cols, contract, 0)
    for z in col_peers:
        sends.append(remote(c_send.at[z], c_recv.at[col], c_s.at[z], c_r.at[col], at_col(z)))
        sends[-1].start()
    total = c_own[col]
    for z in col_peers:
        remote(c_send.at[z], c_recv.at[z], c_s.at[z], c_r.at[z], at_col(z)).wait_recv()
        total = total + c_recv[z].astype(jnp.float32)
    cyc[col, plane] = (scale * total).astype(jnp.bfloat16)

    mine_cyc = cyc.at[col, plane]
    for z in col_peers:
        sends.append(remote(mine_cyc, mine_cyc, az_s.at[z], ag_r.at[col, plane], at_col(z)))
        sends[-1].start()
    for t in plane_peers:
        sends.append(remote(mine_cyc, mine_cyc, ap_s.at[col, t], ag_r.at[col, plane], at_plane(t)))
        sends[-1].start()
    for z in col_peers:
        block = cyc.at[z, plane]
        remote(block, block, az_s.at[z], ag_r.at[z, plane], at_col(z)).wait_recv()
        for t in plane_peers:
            sends.append(remote(block, block, ap_s.at[z, t], ag_r.at[z, plane], at_plane(t)))
            sends[-1].start()
    for t in plane_peers:
        for z in [col] + col_peers:
            block = cyc.at[z, t]
            remote(block, block, ap_s.at[z, t], ag_r.at[z, t], at_plane(t)).wait_recv()
    cyc_out[...] = cyc[...]
    for copy in sends:
        copy.wait_send()


def update_kernel(
    margin_ref, owner_ref, occ_ref, cyc_ref, table_ref, energy_all, energy_ref, amp_ref, k_ref,
    out_ref, term, energy_t,
):
    tables, count = term.shape[0], term.shape[1]
    block, rows = amp_ref.shape[0], amp_ref.shape[1]
    step = pl.program_id(0)
    pairs = energy_all.shape[0]
    first = occ_ref[lax.axis_index("pair")]
    h = lax.axis_index("aux")

    @pl.when(step == 0)
    def _():
        energy_t[...] = energy_all[...].T

        def form(g, carry):
            at = pl.multiple_of(g * 4, 4)
            left = cyc_ref[pl.ds(at, 4)].reshape(4 * rows, 128)
            for m in range(tables):
                value = lax.dot_general(
                    left, table_ref[m], (((1,), (1,)), ((), ())), preferred_element_type=jnp.float32
                )
                term[m, pl.ds(at, 4)] = value.reshape(4, rows, 128)
            return carry

        lax.fori_loop(0, count // 4, form, 0)

    mine = energy_t[pl.ds(pl.multiple_of(h * rows, rows), rows), :]
    mine = pltpu.roll(mine, lax.rem(pairs - step * block, pairs), 1)
    for u in range(block):
        p = step * block + u
        owner = owner_ref[p]
        shift = first + occ_ref[owner]
        across = energy_ref[u : u + 1, :] - shift
        denominator = mine[:, u : u + 1] + across
        inverse = pl.reciprocal(denominator, approx=True)
        inverse = inverse * (2.0 - denominator * inverse)
        numerator = term[margin_ref[p], owner] + k_ref[u].astype(jnp.float32)
        out_ref[u] = (amp_ref[u].astype(jnp.float32) - numerator * inverse).astype(jnp.bfloat16)


def local(
    amplitudes, k_term, margin_table, margin_index, factors, vir_energy, occ_energy, pair_owner
):
    count = lax.axis_size("pair")
    aux_count = lax.axis_size("aux")
    pairs, rows, width = amplitudes.shape
    aux_rows = factors.shape[1]
    tables = margin_table.shape[0]
    planes = 4
    cols = count // planes
    scale = float(width * aux_rows * aux_count * pairs) ** (-0.5)
    bf16, f32 = jnp.bfloat16, jnp.float32

    owner = pair_owner[:, 0]
    slot = (owner % planes) * cols + owner // planes
    key = slot * tables + margin_index
    place = jnp.arange(pairs, dtype=jnp.int32)
    sought = jnp.concatenate([key, jnp.arange(count * tables, dtype=jnp.int32)])
    bound = jnp.concatenate([place, jnp.full((count * tables,), pairs, jnp.int32)])
    hit = (key[None, :] == sought[:, None]) & (place[None, :] < bound[:, None])
    last = jnp.max(jnp.where(hit, place[None, :], -1), axis=1)
    last = jnp.where(last < 0, pairs, last)

    dma = pltpu.SemaphoreType.DMA
    vmem = pl.BlockSpec(memory_space=pltpu.VMEM)
    smem = pl.BlockSpec(memory_space=pltpu.SMEM)
    anywhere = pl.BlockSpec(memory_space=pl.ANY)
    cyc = pl.pallas_call(
        functools.partial(cycle_kernel, (count, planes, cols, tables), scale),
        out_shape=jax.ShapeDtypeStruct((cols, planes, rows, width), bf16),
        in_specs=[smem, anywhere, anywhere, vmem],
        out_specs=vmem,
        scratch_shapes=[
            pltpu.VMEM((pairs, rows, width), bf16),
            pltpu.VMEM((pairs + 1, rows, width), f32),
            pltpu.VMEM((tables, GROUP * rows, width), bf16),
            pltpu.VMEM((tables * rows, GROUP * width), bf16),
            pltpu.VMEM((width, tables * rows), bf16),
            pltpu.VMEM((count, rows, width), bf16),
            pltpu.VMEM((count, rows, width), f32),
            pltpu.VMEM((count, rows, width), bf16),
            pltpu.VMEM((count, rows, width), bf16),
            pltpu.VMEM((planes, cols, rows, width), bf16),
            pltpu.VMEM((planes, aux_rows, width), bf16),
            pltpu.VMEM((cols, aux_rows, width), bf16),
            pltpu.VMEM((cols, planes * width, width), f32),
            pltpu.VMEM((cols, planes * width, width), bf16),
            pltpu.VMEM((cols, planes * width, width), bf16),
            pltpu.VMEM((cols, planes * width, width), bf16),
            pltpu.VMEM((cols, rows, width), f32),
            pltpu.VMEM((cols, rows, width), bf16),
            pltpu.VMEM((cols, rows, width), bf16),
            pltpu.VMEM((cols, planes, rows, width), bf16),
            dma((CHUNKS,)),
            dma((2,)),
            dma((planes,)),
            dma((planes,)),
            dma((cols,)),
            dma((cols,)),
            dma((2,)),
            dma((2,)),
            dma((planes,)),
            dma((planes,)),
            dma((cols,)),
            dma((cols,)),
            dma((cols,)),
            dma((cols, planes)),
            dma((cols, planes)),
        ],
        compiler_params=pltpu.CompilerParams(
            collective_id=0, has_side_effects=True, vmem_limit_bytes=VMEM_BYTES
        ),
        name="cycle",
    )(last, amplitudes, factors, margin_table)

    block = 16
    piece = pl.BlockSpec((block, rows, width), lambda s: (s, 0, 0))
    return pl.pallas_call(
        update_kernel,
        grid=(pairs // block,),
        out_shape=jax.ShapeDtypeStruct(amplitudes.shape, bf16),
        in_specs=[
            smem,
            smem,
            smem,
            vmem,
            vmem,
            vmem,
            pl.BlockSpec((block, width), lambda s: (s, 0)),
            piece,
            piece,
        ],
        out_specs=piece,
        scratch_shapes=[
            pltpu.VMEM((tables, count, rows, width), f32),
            pltpu.VMEM((width, pairs), f32),
        ],
        compiler_params=pltpu.CompilerParams(vmem_limit_bytes=VMEM_BYTES),
        name="update",
    )(
        margin_index, owner, occ_energy, cyc.reshape(count, rows, width), margin_table,
        vir_energy, vir_energy, amplitudes, k_term,
    )


def solution(mesh):
    placed = (
        P("pair", "aux", None),
        P("pair", "aux", None),
        P("pair", None, None),
        P("pair"),
        P("pair", "aux", None),
        P("pair", None),
        P(),
        P("pair", None),
    )
    return jax.shard_map(
        local, mesh=mesh, in_specs=placed, out_specs=P("pair", "aux", None), check_vma=False
    )
```

time: 698 us -> 42.9 us (0.06)
  the two profiles are of different devices: /device:TPU:28 before, /device:TPU:0 now
where the time goes in v1:
time: 42.9 us; the launch traced here: 42.6 us
  Pallas kernels  40.4 us (94%)
  other arithmetic  2.16 us (5%)
    pallas_call x1, Pallas kernels, local(): pl.pallas_call(functools.partial(cycle_kernel, (count, planes, cols, tabl...  31.6 us
    pallas_call x1, Pallas kernels, local(): pl.pallas_call(update_kernel, grid=(pairs // block,), out_shape=jax.Shape...  8.85 us
    reduce_max x1, other arithmetic, local(): last = jnp.max(jnp.where(hit, place[None, :], -1), axis=1)  0.89 us

profile of v1, /device:TPU:0, one launch (start us, length us, event | category | flops | bytes accessed | tf_op | source)
XLA Modules:
  0.0 42.6 jit_solution(767988457175228715)
XLA Ops:
  0.0 0.7 %multiply_add_fusion = s32[128]{0:T(128)S(1)} fusion(s32[128]{0:T(128)} %margin_ref.1, s32[128,1]{0,1:T(1,128)} %param.15), kind=kLoop, calls=%fused_computation.12 | loop fusion | flops 2944 | bytes 1536 | tf_op jit(solution)/shard_map/add | solution.py:247
  0.7 0.9 %select_reduce_fusion = s32[256]{0:T(256)S(1)} fusion(s32[256]{0:T(256)} %constant.37.clone.1, s32[128]{0:T(128)S(1)} %multiply_add_fusion, s32[256]{0:T(256)S(1)} %pad_add_fusion), kind=kLoop, calls=%fused_computation | loop fusion | flops 163584 | bytes 3584 | tf_op jit(solution)/shard_map/reduce_max | solution.py:252
  1.6 0.6 %compare_select_fusion.last_ref = s32[256]{0:T(256)} fusion(s32[256]{0:T(256)S(1)} %select_reduce_fusion), kind=kLoop, calls=%fused_computation.3 | loop fusion | flops 512 | bytes 2048 | tf_op jit(solution)/shard_map/jit(_where)/select_n | solution.py:253
  2.2 31.6 %cycle.1 = bf16[4,4,64,128]{3,2,1,0:T(8,128)(2,1)} custom-call(s32[256]{0:T(256)} %compare_select_fusion.last_ref, bf16[128,64,128]{2,1,0:T(8,128)(2,1)} %amp_ref.1, bf16[1,256,128]{2,1,0:T(8,128)(2,1)} %fac_hbm.1, bf16[8,128,128]{2,1,0:T(8,128)(2,1)} %table_ref.3), custom_call_target="tpu_custom_call" | custom-call | tf_op jit(solution)/shard_map/cycle/pallas_call | solution.py:259
  33.8 8.9 %update.1 = bf16[128,64,128]{2,1,0:T(8,128)(2,1)} custom-call(s32[128]{0:T(128)} %margin_ref.1, s32[128]{0:T(128)} %bitcast.4, f32[16]{0:T(128)} %occ_ref.1, bf16[16,64,128]{2,1,0:T(8,128)(2,1)} %bitcast.3, bf16[8,128,128]{2,1,0:T(8,128)(2,1)} %table_ref.3, f32[128,128]{1,0:T(8,128)} %energy_ref.1, f32[128,128]{1,0:T(8,128)} %energy_ref.1, ...), custom_call_target="tpu_custom_call" | custom-call | tf_op jit(solution)/shard_map/update/pallas_call | solution.py:309
  (2 shorter events, 0.0 us)

commit v2 on v1

v2 whole, which is shorter than its diff:
```python
import functools

import jax
import jax.numpy as jnp
from jax import lax
from jax.experimental import pallas as pl
from jax.experimental.pallas import tpu as pltpu
from jax.sharding import PartitionSpec as P

MESH = pl.DeviceIdType.MESH
VMEM_BYTES = 56 * 1024 * 1024
GROUP = 4
CHUNKS = 4
BLOCK = 16


def dot(a, b):
    return jnp.dot(a, b, preferred_element_type=jnp.float32)


def cycle_kernel(
    sizes, scale,
    last_ref, amp_hbm, fac_hbm, table_ref, cyc_out,
    amp, prefix, half, margin_t, both, r_send, r_own, r_recv, r_sum, r_in,
    f_plane, f_col, g_own, g_send, g_recv, c_own, c_send, c_recv, cyc,
    amp_sem, loc_sem, fp_s, fp_r, fz_s, fz_r, sr_s, sr_r, sg_s, sg_r, r_s, r_r, c_s, c_r,
    az_s, ap_s, ag_r,
):
    count, planes, cols, tables = sizes
    rows = amp.shape[1]
    pairs = amp.shape[0]
    me, h = lax.axis_index("pair"), lax.axis_index("aux")
    col, plane = lax.div(me, planes), lax.rem(me, planes)
    sibling = (me, 1 - h)
    plane_peers = [lax.rem(plane + d, planes) for d in range(1, planes)]
    col_peers = [lax.rem(col + d, cols) for d in range(1, cols)]

    def at_plane(t):
        return (col * planes + t, h)

    def at_col(z):
        return (z * planes + plane, h)

    def remote(src, dst, send, recv, device):
        return pltpu.make_async_remote_copy(
            src_ref=src, dst_ref=dst, send_sem=send, recv_sem=recv,
            device_id=device, device_id_type=MESH,
        )

    step = pairs // CHUNKS
    loads = []
    for k in range(CHUNKS):
        part = pl.ds(k * step, step)
        loads.append(pltpu.make_async_copy(amp_hbm.at[part], amp.at[part], amp_sem.at[k]))
        loads[-1].start()
    own_plane = pltpu.make_async_copy(fac_hbm.at[0], f_plane.at[plane], loc_sem.at[0])
    own_col = pltpu.make_async_copy(fac_hbm.at[0], f_col.at[col], loc_sem.at[1])
    own_plane.start()
    own_col.start()

    barrier = pltpu.get_barrier_semaphore()
    for device in [sibling] + [at_plane(t) for t in plane_peers] + [at_col(z) for z in col_peers]:
        pl.semaphore_signal(barrier, inc=1, device_id=device, device_id_type=MESH)
    pl.semaphore_wait(barrier, 1 + (planes - 1) + (cols - 1))

    sends = []
    for z in col_peers:
        sends.append(remote(fac_hbm.at[0], f_col.at[col], fz_s.at[z], fz_r.at[col], at_col(z)))
        sends[-1].start()
    for t in plane_peers:
        sends.append(remote(fac_hbm.at[0], f_plane.at[plane], fp_s.at[t], fp_r.at[plane], at_plane(t)))
        sends[-1].start()

    prefix[0] = jnp.zeros(prefix.shape[1:], jnp.float32)
    for m in range(tables):
        piece = table_ref[m, pl.ds(pl.multiple_of(h * rows, rows), rows), :]
        margin_t[:, m * rows : (m + 1) * rows] = piece.T
    both[0:rows] = margin_t[pl.ds(pl.multiple_of((1 - h) * rows, rows), rows), :]
    both[rows : 2 * rows] = margin_t[pl.ds(pl.multiple_of(h * rows, rows), rows), :]

    for k in range(CHUNKS):
        loads[k].wait()

        def add_pair(p, carry):
            prefix[p + 1] = amp[p].astype(jnp.float32) + prefix[last_ref[p]]
            return carry

        lax.fori_loop(k * step, (k + 1) * step, add_pair, 0, unroll=8)

    def rotate(base, held):
        for m in range(tables):
            found = [prefix[last_ref[pairs + (base + u) * tables + m]] for u in range(GROUP)]
            value = dot(jnp.concatenate(found, axis=0).astype(jnp.bfloat16), table_ref[m])
            value = value.astype(jnp.bfloat16)
            for u in range(GROUP):
                held[m * rows : (m + 1) * rows, u * 128 : (u + 1) * 128] = value[
                    u * rows : (u + 1) * rows
                ]
        for u in range(0, GROUP, 2):
            value = dot(both[...], held[:, u * 128 : (u + 2) * 128])
            for v in range(2):
                turned = value[:, v * 128 : (v + 1) * 128]
                r_send[base + u + v] = turned[0:rows].astype(jnp.bfloat16)
                r_own[base + u + v] = turned[rows : 2 * rows]

    def swap_piece(t):
        piece = pl.ds(t * cols, cols)
        return remote(r_send.at[piece], r_recv.at[piece], sr_s.at[t], sr_r.at[t], sibling)

    def add_piece(t):
        swap_piece(t).wait()
        piece = pl.ds(t * cols, cols)
        return (r_own[piece] + r_recv[piece].astype(jnp.float32)).astype(jnp.bfloat16)

    def send_piece(t):
        r_sum[t] = add_piece(t)
        sends.append(remote(r_sum.at[t], r_in.at[plane], r_s.at[t], r_r.at[plane], at_plane(t)))
        sends[-1].start()

    for d, t in enumerate(plane_peers + [plane]):
        held = half.at[d % 2]
        if cols == GROUP:
            rotate(t * cols, held)
        else:
            lax.fori_loop(
                0, cols // GROUP, lambda g, carry: rotate(t * cols + g * GROUP, held) or carry, 0
            )
        swap_piece(t).start()
        if d >= 1:
            send_piece(plane_peers[d - 1])

    own_plane.wait()
    own_col.wait()
    for t in plane_peers:
        remote(fac_hbm.at[0], f_plane.at[t], fp_s.at[t], fp_r.at[t], at_plane(t)).wait_recv()

    def swap_metric(z):
        return remote(g_send.at[z], g_recv.at[z], sg_s.at[z], sg_r.at[z], sibling)

    turned = [f_plane[s].T for s in range(planes)]
    for z in [col] + col_peers:
        if z is not col:
            remote(fac_hbm.at[0], f_col.at[z], fz_s.at[z], fz_r.at[z], at_col(z)).wait_recv()
        for s in range(planes):
            value = dot(turned[s], f_col[z])
            g_own[z, s * 128 : (s + 1) * 128, :] = value
            g_send[z, s * 128 : (s + 1) * 128, :] = value.astype(jnp.bfloat16)
        swap_metric(z).start()

    r_in[plane] = add_piece(plane)
    for t in plane_peers:
        remote(r_sum.at[t], r_in.at[t], r_s.at[t], r_r.at[t], at_plane(t)).wait_recv()

    for z in col_peers + [col]:
        swap_metric(z).wait()
        whole = (g_own[z] + g_recv[z].astype(jnp.float32)).astype(jnp.bfloat16)
        value = dot(jnp.concatenate([r_in[s, z] for s in range(planes)], axis=1), whole)
        if z is col:
            c_own[...] = value
        else:
            c_send[z] = value.astype(jnp.bfloat16)
            sends.append(remote(c_send.at[z], c_recv.at[col], c_s.at[z], c_r.at[col], at_col(z)))
            sends[-1].start()
    total = c_own[...]
    for z in col_peers:
        remote(c_send.at[z], c_recv.at[z], c_s.at[z], c_r.at[z], at_col(z)).wait_recv()
        total = total + c_recv[z].astype(jnp.float32)
    cyc[col, plane] = (scale * total).astype(jnp.bfloat16)

    mine_cyc = cyc.at[col, plane]
    for z in col_peers:
        sends.append(remote(mine_cyc, mine_cyc, az_s.at[z], ag_r.at[col, plane], at_col(z)))
        sends[-1].start()
    for t in plane_peers:
        sends.append(remote(mine_cyc, mine_cyc, ap_s.at[col, t], ag_r.at[col, plane], at_plane(t)))
        sends[-1].start()
    for z in col_peers:
        block = cyc.at[z, plane]
        remote(block, block, az_s.at[z], ag_r.at[z, plane], at_col(z)).wait_recv()
        for t in plane_peers:
            sends.append(remote(block, block, ap_s.at[z, t], ag_r.at[z, plane], at_plane(t)))
            sends[-1].start()
    for t in plane_peers:
        for z in [col] + col_peers:
            block = cyc.at[z, t]
            remote(block, block, ap_s.at[z, t], ag_r.at[z, t], at_plane(t)).wait_recv()
    cyc_out[...] = cyc[...]
    for copy in sends:
        copy.wait_send()


def update_kernel(
    margin_ref, owner_ref, occ_ref, cyc_ref, table_ref, energy_ref, amp_hbm, k_hbm,
    out_hbm, term, energy_t, amp, k_held, out, amp_sem, k_sem, out_sem,
):
    tables, count = term.shape[0], term.shape[1]
    pairs, rows = amp.shape[0], amp.shape[1]
    first = occ_ref[lax.axis_index("pair")]
    h = lax.axis_index("aux")

    def load(s):
        part = pl.ds(s * BLOCK, BLOCK)
        return (
            pltpu.make_async_copy(amp_hbm.at[part], amp.at[part], amp_sem.at[s]),
            pltpu.make_async_copy(k_hbm.at[part], k_held.at[part], k_sem.at[s]),
        )

    def store(s):
        part = pl.ds(s * BLOCK, BLOCK)
        return pltpu.make_async_copy(out.at[part], out_hbm.at[part], out_sem.at[s])

    for s in range(pairs // BLOCK):
        for copy in load(s):
            copy.start()

    energy_t[...] = energy_ref[...].T

    def form(g, carry):
        at = pl.multiple_of(g * 8, 8)
        left = cyc_ref[pl.ds(at, 8)].reshape(8 * rows, 128)
        for m in range(0, tables, 2):
            right = table_ref[m : m + 2].reshape(256, 128)
            value = lax.dot_general(
                left, right, (((1,), (1,)), ((), ())), preferred_element_type=jnp.float32
            )
            for v in range(2):
                term[m + v, pl.ds(at, 8)] = value[:, v * 128 : (v + 1) * 128].reshape(8, rows, 128)
        return carry

    lax.fori_loop(0, count // 8, form, 0)

    def renew(s, carry):
        for copy in load(s):
            copy.wait()
        mine = energy_t[pl.ds(pl.multiple_of(h * rows, rows), rows), :]
        mine = pltpu.roll(mine, lax.rem(pairs - s * BLOCK, pairs), 1)
        for u in range(BLOCK):
            p = s * BLOCK + u
            owner = owner_ref[p]
            across = energy_ref[pl.ds(p, 1), :] - (first + occ_ref[owner])
            denominator = mine[:, u : u + 1] + across
            inverse = pl.reciprocal(denominator, approx=True)
            inverse = inverse * (2.0 - denominator * inverse)
            numerator = term[margin_ref[p], owner] + k_held[p].astype(jnp.float32)
            out[p] = (amp[p].astype(jnp.float32) - numerator * inverse).astype(jnp.bfloat16)
        store(s).start()
        return carry

    lax.fori_loop(0, pairs // BLOCK, renew, 0)
    for s in range(pairs // BLOCK):
        store(s).wait()


def local(
    amplitudes, k_term, margin_table, margin_index, factors, vir_energy, occ_energy, pair_owner
):
    count = lax.axis_size("pair")
    aux_count = lax.axis_size("aux")
    pairs, rows, width = amplitudes.shape
    aux_rows = factors.shape[1]
    tables = margin_table.shape[0]
    planes = 4
    cols = count // planes
    scale = float(width * aux_rows * aux_count * pairs) ** (-0.5)
    bf16, f32 = jnp.bfloat16, jnp.float32

    owner = pair_owner[:, 0]
    slot = (owner % planes) * cols + owner // planes
    key = slot * tables + margin_index
    place = jnp.arange(pairs, dtype=jnp.int32)
    sought = jnp.concatenate([key, jnp.arange(count * tables, dtype=jnp.int32)])
    bound = jnp.concatenate([place, jnp.full((count * tables,), pairs, jnp.int32)])
    hit = (key[None, :] == sought[:, None]) & (place[None, :] < bound[:, None])
    last = jnp.max(jnp.where(hit, place[None, :] + 1, 0), axis=1)

    dma = pltpu.SemaphoreType.DMA
    vmem = pl.BlockSpec(memory_space=pltpu.VMEM)
    smem = pl.BlockSpec(memory_space=pltpu.SMEM)
    anywhere = pl.BlockSpec(memory_space=pl.ANY)
    cyc = pl.pallas_call(
        functools.partial(cycle_kernel, (count, planes, cols, tables), scale),
        out_shape=jax.ShapeDtypeStruct((cols, planes, rows, width), bf16),
        in_specs=[smem, anywhere, anywhere, vmem],
        out_specs=vmem,
        scratch_shapes=[
            pltpu.VMEM((pairs, rows, width), bf16),
            pltpu.VMEM((pairs + 1, rows, width), f32),
            pltpu.VMEM((2, tables * rows, GROUP * width), bf16),
            pltpu.VMEM((width, tables * rows), bf16),
            pltpu.VMEM((2 * rows, tables * rows), bf16),
            pltpu.VMEM((count, rows, width), bf16),
            pltpu.VMEM((count, rows, width), f32),
            pltpu.VMEM((count, rows, width), bf16),
            pltpu.VMEM((planes, cols, rows, width), bf16),
            pltpu.VMEM((planes, cols, rows, width), bf16),
            pltpu.VMEM((planes, aux_rows, width), bf16),
            pltpu.VMEM((cols, aux_rows, width), bf16),
            pltpu.VMEM((cols, planes * width, width), f32),
            pltpu.VMEM((cols, planes * width, width), bf16),
            pltpu.VMEM((cols, planes * width, width), bf16),
            pltpu.VMEM((rows, width), f32),
            pltpu.VMEM((cols, rows, width), bf16),
            pltpu.VMEM((cols, rows, width), bf16),
            pltpu.VMEM((cols, planes, rows, width), bf16),
            dma((CHUNKS,)),
            dma((2,)),
            dma((planes,)),
            dma((planes,)),
            dma((cols,)),
            dma((cols,)),
            dma((planes,)),
            dma((planes,)),
            dma((cols,)),
            dma((cols,)),
            dma((planes,)),
            dma((planes,)),
            dma((cols,)),
            dma((cols,)),
            dma((cols,)),
            dma((cols, planes)),
            dma((cols, planes)),
        ],
        compiler_params=pltpu.CompilerParams(
            collective_id=0, has_side_effects=True, vmem_limit_bytes=VMEM_BYTES
        ),
        name="cycle",
    )(last, amplitudes, factors, margin_table)

    whole = pltpu.VMEM((pairs, rows, width), bf16)
    return pl.pallas_call(
        update_kernel,
        out_shape=jax.ShapeDtypeStruct(amplitudes.shape, bf16),
        in_specs=[smem, smem, smem, vmem, vmem, vmem, anywhere, anywhere],
        out_specs=anywhere,
        scratch_shapes=[
            pltpu.VMEM((tables, count, rows, width), f32),
            pltpu.VMEM((width, pairs), f32),
            whole,
            whole,
            whole,
            dma((pairs // BLOCK,)),
            dma((pairs // BLOCK,)),
            dma((pairs // BLOCK,)),
        ],
        compiler_params=pltpu.CompilerParams(vmem_limit_bytes=VMEM_BYTES),
        name="update",
    )(
        margin_index, owner, occ_energy, cyc.reshape(count, rows, width), margin_table,
        vir_energy, amplitudes, k_term,
    )


def solution(mesh):
    placed = (
        P("pair", "aux", None),
        P("pair", "aux", None),
        P("pair", None, None),
        P("pair"),
        P("pair", "aux", None),
        P("pair", None),
        P(),
        P("pair", None),
    )
    return jax.shard_map(
        local, mesh=mesh, in_specs=placed, out_specs=P("pair", "aux", None), check_vma=False
    )
```

time: 42.9 us -> 35.1 us (0.82)
  Pallas kernels: 40.4 us -> 32.8 us
    pallas_call x1, Pallas kernels: 31.6 us -> 27.3 us  [local(): pl.pallas_call(functools.partial(cycle_kernel, (count, planes, cols, tabl...]
    pallas_call x1, Pallas kernels: 8.85 us -> 5.53 us  [local(): pl.pallas_call(update_kernel, out_shape=jax.ShapeDtypeStruct(amplitudes.s...]
    select_n x1 -> x0, other arithmetic: 0.57 us -> none  [local(): last = jnp.where(last < 0, pairs, last)]
    reduce_max x1, other arithmetic: 0.89 us -> 1.46 us  [local(): last = jnp.max(jnp.where(hit, place[None, :] + 1, 0), axis=1)]
where the time goes in v2:
time: 35.1 us; the launch traced here: 35 us
  Pallas kernels  32.8 us (93%)
  other arithmetic  2.15 us (6%)
    pallas_call x1, Pallas kernels, local(): pl.pallas_call(functools.partial(cycle_kernel, (count, planes, cols, tabl...  27.3 us
    pallas_call x1, Pallas kernels, local(): pl.pallas_call(update_kernel, out_shape=jax.ShapeDtypeStruct(amplitudes.s...  5.53 us
    reduce_max x1, other arithmetic, local(): last = jnp.max(jnp.where(hit, place[None, :] + 1, 0), axis=1)  1.46 us

profile of v2, /device:TPU:0, one launch (start us, length us, event | category | flops | bytes accessed | tf_op | source)
XLA Modules:
  0.0 35.0 jit_solution(3010515207819294065)
XLA Ops:
  0.0 0.7 %iota_add_fusion = (s32[128]{0:T(128)S(1)}, s32[128]{0:T(128)S(1)}) fusion(s32[128]{0:T(128)} %margin_ref.1, s32[128,1]{0,1:T(1,128)} %param.15), kind=kLoop, calls=%fused_computation.11 | loop fusion | flops 3072 | bytes 2048 | tf_op jit(solution)/shard_map/add | solution.py:274
  0.7 1.5 %select_reduce_fusion.last_ref = s32[256]{0:T(256)} fusion(s32[128]{0:T(128)S(1)} %get-tuple-element.5, s32[256]{0:T(256)} %constant.36.clone.1, s32[128]{0:T(128)S(1)} %get-tuple-element.6, s32[256]{0:T(256)S(1)} %pad_add_fusion), kind=kLoop, calls=%fused_computation | loop fusion | flops 163584 | bytes 4096 | tf_op jit(solution)/shard_map/reduce_max | solution.py:274
  2.2 27.3 %cycle.1 = bf16[4,4,64,128]{3,2,1,0:T(8,128)(2,1)} custom-call(s32[256]{0:T(256)} %select_reduce_fusion.last_ref, bf16[128,64,128]{2,1,0:T(8,128)(2,1)} %amp_hbm.3, bf16[1,256,128]{2,1,0:T(8,128)(2,1)} %fac_hbm.1, bf16[8,128,128]{2,1,0:T(8,128)(2,1)} %table_ref.3), custom_call_target="tpu_custom_call" | custom-call | tf_op jit(solution)/shard_map/cycle/pallas_call | solution.py:280
  29.4 5.5 %update.1 = bf16[128,64,128]{2,1,0:T(8,128)(2,1)} custom-call(s32[128]{0:T(128)} %margin_ref.1, s32[128]{0:T(128)} %bitcast.4, f32[16]{0:T(128)} %occ_ref.1, bf16[16,64,128]{2,1,0:T(8,128)(2,1)} %bitcast.3, bf16[8,128,128]{2,1,0:T(8,128)(2,1)} %table_ref.3, f32[128,128]{1,0:T(8,128)} %energy_ref.1, bf16[128,64,128]{2,1,0:T(8,128)(2,1)} %amp_hbm.3, ...), custom_call_target="tpu_custom_call" | custom-call | tf_op jit(solution)/shard_map/update/pallas_call | solution.py:330
  (2 shorter events, 0.0 us)

commit v3 on v2

--- a/solution.py
+++ b/solution.py
@@ -8,7 +8,6 @@
 from jax.sharding import PartitionSpec as P
 
 MESH = pl.DeviceIdType.MESH
-VMEM_BYTES = 56 * 1024 * 1024
 GROUP = 4
 CHUNKS = 4
 BLOCK = 16
@@ -117,7 +116,7 @@
         sends.append(remote(r_sum.at[t], r_in.at[plane], r_s.at[t], r_r.at[plane], at_plane(t)))
         sends[-1].start()
 
-    for d, t in enumerate(plane_peers + [plane]):
+    def rotate_all(d, t):
         held = half.at[d % 2]
         if cols == GROUP:
             rotate(t * cols, held)
@@ -126,6 +125,9 @@
                 0, cols // GROUP, lambda g, carry: rotate(t * cols + g * GROUP, held) or carry, 0
             )
         swap_piece(t).start()
+
+    for d, t in enumerate(plane_peers):
+        rotate_all(d, t)
         if d >= 1:
             send_piece(plane_peers[d - 1])
 
@@ -146,7 +148,10 @@
             g_own[z, s * 128 : (s + 1) * 128, :] = value
             g_send[z, s * 128 : (s + 1) * 128, :] = value.astype(jnp.bfloat16)
         swap_metric(z).start()
-
+        if z is col:
+            send_piece(plane_peers[-1])
+
+    rotate_all(planes - 1, plane)
     r_in[plane] = add_piece(plane)
     for t in plane_peers:
         remote(r_sum.at[t], r_in.at[t], r_s.at[t], r_r.at[t], at_plane(t)).wait_recv()
@@ -263,6 +268,7 @@
     cols = count // planes
     scale = float(width * aux_rows * aux_count * pairs) ** (-0.5)
     bf16, f32 = jnp.bfloat16, jnp.float32
+    vmem_bytes = min(56 << 20, (14 << 20) + count * (3 << 17))
 
     owner = pair_owner[:, 0]
     slot = (owner % planes) * cols + owner // planes
@@ -270,8 +276,8 @@
     place = jnp.arange(pairs, dtype=jnp.int32)
     sought = jnp.concatenate([key, jnp.arange(count * tables, dtype=jnp.int32)])
     bound = jnp.concatenate([place, jnp.full((count * tables,), pairs, jnp.int32)])
-    hit = (key[None, :] == sought[:, None]) & (place[None, :] < bound[:, None])
-    last = jnp.max(jnp.where(hit, place[None, :] + 1, 0), axis=1)
+    hit = (key[:, None] == sought[None, :]) & (place[:, None] < bound[None, :])
+    last = jnp.max(jnp.where(hit, place[:, None] + 1, 0), axis=0)
 
     dma = pltpu.SemaphoreType.DMA
     vmem = pl.BlockSpec(memory_space=pltpu.VMEM)
@@ -321,7 +327,7 @@
             dma((cols, planes)),
         ],
         compiler_params=pltpu.CompilerParams(
-            collective_id=0, has_side_effects=True, vmem_limit_bytes=VMEM_BYTES
+            collective_id=0, has_side_effects=True, vmem_limit_bytes=vmem_bytes
         ),
         name="cycle",
     )(last, amplitudes, factors, margin_table)
@@ -342,7 +348,7 @@
             dma((pairs // BLOCK,)),
             dma((pairs // BLOCK,)),
         ],
-        compiler_params=pltpu.CompilerParams(vmem_limit_bytes=VMEM_BYTES),
+        compiler_params=pltpu.CompilerParams(vmem_limit_bytes=vmem_bytes),
         name="update",
     )(
         margin_index, owner, occ_energy, cyc.reshape(count, rows, width), margin_table,

time: 35.1 us -> 39.3 us (1.12)
  local copies, waits for them, and re-layouts: 0.01 us -> 4.99 us
  other arithmetic: 2.15 us -> 1.54 us
  Pallas kernels: 32.8 us -> 32.4 us
    unnamed x0 -> x20, local copies, waits for them, and re-layouts: none -> 4.98 us
    reduce_max x1, other arithmetic: 1.46 us -> 0.79 us  [local(): last = jnp.max(jnp.where(hit, place[:, None] + 1, 0), axis=0)]
where the time goes in v3:
time: 39.3 us; the launch traced here: 39 us
  Pallas kernels  32.4 us (82%)
  local copies, waits for them, and re-layouts  4.99 us (13%)
  other arithmetic  1.54 us (4%)
    pallas_call x1, Pallas kernels, local(): pl.pallas_call(functools.partial(cycle_kernel, (count, planes, cols, tabl...  27.1 us
    pallas_call x1, Pallas kernels, local(): pl.pallas_call(update_kernel, out_shape=jax.ShapeDtypeStruct(amplitudes.s...  5.28 us
    unnamed x20, local copies, waits for them, and re-layouts  4.98 us
    reduce_max x1, other arithmetic, local(): last = jnp.max(jnp.where(hit, place[:, None] + 1, 0), axis=0)  0.79 us

profile of v3, /device:TPU:0, one launch (start us, length us, event | category | flops | bytes accessed | tf_op | source)
XLA Modules:
  0.0 39.0 jit_solution(3201566020905259327)
XLA Ops:
  0.0 0.0 copy-start.8
  0.0 0.0 copy-start.7
  0.0 0.0 copy-start.9
  0.0 0.7 %iota_add_fusion = (s32[128]{0:T(128)S(1)}, s32[128]{0:T(128)S(1)}) fusion(s32[128]{0:T(128)} %margin_ref.1, s32[128,1]{0,1:T(1,128)} %param.15), kind=kLoop, calls=%fused_computation.11 | loop fusion | flops 3072 | bytes 2048 | tf_op jit(solution)/shard_map/add | solution.py:280
  0.8 0.8 %select_reduce_fusion.last_ref = s32[256]{0:T(256)S(1)} fusion(s32[128]{0:T(128)S(1)} %get-tuple-element.5, s32[256]{0:T(256)} %constant.36.clone.1, s32[256]{0:T(256)S(1)} %pad_add_fusion, s32[128]{0:T(128)S(1)} %get-tuple-element.6), kind=kLoop, calls=%fused_computation | loop fusion | flops 163584 | bytes 4096 | tf_op jit(solution)/shard_map/reduce_max | solution.py:280
  1.6 0.0 copy-start
  1.6 1.6 %copy-done = bf16[128,64,128]{2,1,0:T(8,128)(2,1)S(1)} copy-done((bf16[128,64,128]{2,1,0:T(8,128)(2,1)S(1)}, bf16[128,64,128]{2,1,0:T(8,128)(2,1)}, u32[]{:S(2)}) %copy-start) | copy-done | bytes 2097176
  3.2 0.0 copy-start.3
  3.2 0.9 %copy-done.3 = bf16[8,128,128]{2,1,0:T(8,128)(2,1)S(1)} copy-done((bf16[8,128,128]{2,1,0:T(8,128)(2,1)S(1)}, bf16[8,128,128]{2,1,0:T(8,128)(2,1)}, u32[]{:S(2)}) %copy-start.3) | copy-done | bytes 262168
  4.1 0.0 copy-start.6
  4.1 0.8 %copy-done.6 = bf16[1,256,128]{2,1,0:T(8,128)(2,1)S(1)} copy-done((bf16[1,256,128]{2,1,0:T(8,128)(2,1)S(1)}, bf16[1,256,128]{2,1,0:T(8,128)(2,1)}, u32[]{:S(2)}) %copy-start.6) | copy-done | bytes 65560
  4.9 0.0 copy-start.1
  4.9 0.0 copy-start.4
  4.9 0.0 copy-start.5
  4.9 27.1 %cycle.1 = bf16[4,4,64,128]{3,2,1,0:T(8,128)(2,1)S(1)} custom-call(s32[256]{0:T(256)S(1)} %select_reduce_fusion.last_ref, bf16[128,64,128]{2,1,0:T(8,128)(2,1)S(1)} %copy-done, bf16[1,256,128]{2,1,0:T(8,128)(2,1)S(1)} %copy-done.6, bf16[8,128,128]{2,1,0:T(8,128)(2,1)S(1)} %copy-done.3), custom_call_target="tpu_custom_call" | custom-call | tf_op jit(solution)/shard_map/cycle/pallas_call | solution.py:286
  32.1 0.0 copy-done.8
  32.1 0.0 copy-done.7
  32.1 0.0 copy-done.9
  32.1 0.0 copy-done.1
  32.1 0.0 copy-done.4
  32.1 0.0 copy-done.5
  32.1 0.0 copy-start.2
  32.1 1.6 %copy-done.2 = bf16[128,64,128]{2,1,0:T(8,128)(2,1)S(1)} copy-done((bf16[128,64,128]{2,1,0:T(8,128)(2,1)S(1)}, bf16[128,64,128]{2,1,0:T(8,128)(2,1)}, u32[]{:S(2)}) %copy-start.2) | copy-done | bytes 2097176
  33.7 5.3 %update.1 = bf16[128,64,128]{2,1,0:T(8,128)(2,1)} custom-call(s32[128]{0:T(128)S(1)} %copy-done.7, s32[128]{0:T(128)S(1)} %bitcast.4, f32[16]{0:T(128)S(1)} %copy-done.9, bf16[16,64,128]{2,1,0:T(8,128)(2,1)S(1)} %bitcast.3, bf16[8,128,128]{2,1,0:T(8,128)(2,1)S(1)} %copy-done.4, f32[128,128]{1,0:T(8,128)S(1)} %copy-done.5, ...), custom_call_target="tpu_custom_call" | custom-call | tf_op jit(solution)/shard_map/update/pallas_call | solution.py:336
  (2 shorter events, 0.0 us)
Async XLA Ops:
  0.0 32.1 %copy-start.8 = (s32[128,1]{0,1:T(1,128)S(1)}, s32[128,1]{0,1:T(1,128)}, u32[]{:S(2)}) copy-start(s32[128,1]{0,1:T(1,128)} %param.15) | copy-start | bytes 1540
  0.0 32.1 %copy-start.7 = (s32[128]{0:T(128)S(1)}, s32[128]{0:T(128)}, u32[]{:S(2)}) copy-start(s32[128]{0:T(128)} %margin_ref.1) | copy-start | bytes 1540
  0.0 32.1 %copy-start.9 = (f32[16]{0:T(128)S(1)}, f32[16]{0:T(128)}, u32[]{:S(2)}) copy-start(f32[16]{0:T(128)} %occ_ref.1) | copy-start | bytes 196
  1.6 1.6 %copy-start = (bf16[128,64,128]{2,1,0:T(8,128)(2,1)S(1)}, bf16[128,64,128]{2,1,0:T(8,128)(2,1)}, u32[]{:S(2)}) copy-start(bf16[128,64,128]{2,1,0:T(8,128)(2,1)} %amp_hbm.3) | copy-start | bytes 6291460
  3.2 0.9 %copy-start.3 = (bf16[8,128,128]{2,1,0:T(8,128)(2,1)S(1)}, bf16[8,128,128]{2,1,0:T(8,128)(2,1)}, u32[]{:S(2)}) copy-start(bf16[8,128,128]{2,1,0:T(8,128)(2,1)} %table_ref.3) | copy-start | bytes 786436
  4.1 0.8 %copy-start.6 = (bf16[1,256,128]{2,1,0:T(8,128)(2,1)S(1)}, bf16[1,256,128]{2,1,0:T(8,128)(2,1)}, u32[]{:S(2)}) copy-start(bf16[1,256,128]{2,1,0:T(8,128)(2,1)} %fac_hbm.1) | copy-start | bytes 196612
  4.9 27.2 %copy-start.1 = (bf16[128,64,128]{2,1,0:T(8,128)(2,1)S(1)}, bf16[128,64,128]{2,1,0:T(8,128)(2,1)}, u32[]{:S(2)}) copy-start(bf16[128,64,128]{2,1,0:T(8,128)(2,1)} %amp_hbm.3) | copy-start | bytes 6291460
  4.9 27.2 %copy-start.4 = (bf16[8,128,128]{2,1,0:T(8,128)(2,1)S(1)}, bf16[8,128,128]{2,1,0:T(8,128)(2,1)}, u32[]{:S(2)}) copy-start(bf16[8,128,128]{2,1,0:T(8,128)(2,1)} %table_ref.3) | copy-start | bytes 786436
  4.9 27.2 %copy-start.5 = (f32[128,128]{1,0:T(8,128)S(1)}, f32[128,128]{1,0:T(8,128)}, u32[]{:S(2)}) copy-start(f32[128,128]{1,0:T(8,128)} %energy_ref.1) | copy-start | bytes 196612
  32.1 1.6 %copy-start.2 = (bf16[128,64,128]{2,1,0:T(8,128)(2,1)S(1)}, bf16[128,64,128]{2,1,0:T(8,128)(2,1)}, u32[]{:S(2)}) copy-start(bf16[128,64,128]{2,1,0:T(8,128)(2,1)} %k_hbm.1) | copy-start | bytes 6291460

commit v4 on v3

--- a/solution.py
+++ b/solution.py
@@ -268,7 +268,7 @@
     cols = count // planes
     scale = float(width * aux_rows * aux_count * pairs) ** (-0.5)
     bf16, f32 = jnp.bfloat16, jnp.float32
-    vmem_bytes = min(56 << 20, (14 << 20) + count * (3 << 17))
+    vmem_bytes = 56 << 20
 
     owner = pair_owner[:, 0]
     slot = (owner % planes) * cols + owner // planes

time: 39.3 us -> 35.8 us (0.911)
  local copies, waits for them, and re-layouts: 4.99 us -> 0.01 us
  Pallas kernels: 32.4 us -> 33.6 us
  other arithmetic: 1.54 us -> 2.05 us
    unnamed x20 -> x0, local copies, waits for them, and re-layouts: 4.98 us -> none
    pallas_call x1, Pallas kernels: 27.1 us -> 28 us  [local(): pl.pallas_call(functools.partial(cycle_kernel, (count, planes, cols, tabl...]
    reduce_max x1, other arithmetic: 0.79 us -> 1.36 us  [local(): last = jnp.max(jnp.where(hit, place[:, None] + 1, 0), axis=0)]
where the time goes in v4:
time: 35.8 us; the launch traced here: 35.6 us
  Pallas kernels  33.6 us (94%)
  other arithmetic  2.05 us (6%)
    pallas_call x1, Pallas kernels, local(): pl.pallas_call(functools.partial(cycle_kernel, (count, planes, cols, tabl...  28 us
    pallas_call x1, Pallas kernels, local(): pl.pallas_call(update_kernel, out_shape=jax.ShapeDtypeStruct(amplitudes.s...  5.53 us
    reduce_max x1, other arithmetic, local(): last = jnp.max(jnp.where(hit, place[:, None] + 1, 0), axis=0)  1.36 us

profile of v4, /device:TPU:0, one launch (start us, length us, event | category | flops | bytes accessed | tf_op | source)
XLA Modules:
  0.0 35.6 jit_solution(17349289464630764826)
XLA Ops:
  0.0 0.7 %iota_add_fusion = (s32[128]{0:T(128)S(1)}, s32[128]{0:T(128)S(1)}) fusion(s32[128]{0:T(128)} %margin_ref.1, s32[128,1]{0,1:T(1,128)} %param.15), kind=kLoop, calls=%fused_computation.11 | loop fusion | flops 3072 | bytes 2048 | tf_op jit(solution)/shard_map/add | solution.py:280
  0.7 1.4 %select_reduce_fusion.last_ref = s32[256]{0:T(256)} fusion(s32[128]{0:T(128)S(1)} %get-tuple-element.5, s32[256]{0:T(256)} %constant.36.clone.1, s32[256]{0:T(256)S(1)} %pad_add_fusion, s32[128]{0:T(128)S(1)} %get-tuple-element.6), kind=kLoop, calls=%fused_computation | loop fusion | flops 163584 | bytes 4096 | tf_op jit(solution)/shard_map/reduce_max | solution.py:280
  2.1 28.0 %cycle.1 = bf16[4,4,64,128]{3,2,1,0:T(8,128)(2,1)} custom-call(s32[256]{0:T(256)} %select_reduce_fusion.last_ref, bf16[128,64,128]{2,1,0:T(8,128)(2,1)} %amp_hbm.3, bf16[1,256,128]{2,1,0:T(8,128)(2,1)} %fac_hbm.1, bf16[8,128,128]{2,1,0:T(8,128)(2,1)} %table_ref.3), custom_call_target="tpu_custom_call" | custom-call | tf_op jit(solution)/shard_map/cycle/pallas_call | solution.py:286
  30.1 5.5 %update.1 = bf16[128,64,128]{2,1,0:T(8,128)(2,1)} custom-call(s32[128]{0:T(128)} %margin_ref.1, s32[128]{0:T(128)} %bitcast.4, f32[16]{0:T(128)} %occ_ref.1, bf16[16,64,128]{2,1,0:T(8,128)(2,1)} %bitcast.3, bf16[8,128,128]{2,1,0:T(8,128)(2,1)} %table_ref.3, f32[128,128]{1,0:T(8,128)} %energy_ref.1, bf16[128,64,128]{2,1,0:T(8,128)(2,1)} %amp_hbm.3, ...), custom_call_target="tpu_custom_call" | custom-call | tf_op jit(solution)/shard_map/update/pallas_call | solution.py:336
  (2 shorter events, 0.0 us)
